TPU v7x, 32 devices: a whole 2x2x4 slice. The times are simulated.
32 devices in a mesh: groups: 2 (over x), rows: 8 (over z, y), cls: 2 (over core).
Axes of the slice: x: 2, y: 2, z: 4, core: 2. Of those that a mesh axis runs over, the one named last changes fastest.
Arguments:
- embeddings: bfloat16 [8192, 1024], P(('groups', 'rows')), parts along dimension 0, may hold values from -6 to 6
- omega: bfloat16 [1024, 3072], replicated, may hold values from -0.25 to 0.25
- phases: float32 [3072], replicated, may hold values from -3.140625 to 3.140625
- index_list: int32 [3072], replicated, may hold values from 0 to 3071, each once
- inverse_store: bfloat16 [16, 1024, 1024], P(('groups', 'rows')), parts along dimension 0, as said below
- roots: int32 [3], replicated, may hold values from 0 to 7, as said below
- residual_in: bfloat16 [8192, 1024], P(('groups', 'rows'), 'cls'), parts along dimension 0, may hold values from -6 to 6
Outputs:
- changes: bfloat16 [6, 1024, 1024], P('groups', None, 'cls'), parts along dimension 0
- residual_out: bfloat16 [8192, 1024], P(('groups', 'rows'), 'cls'), parts along dimension 0
There are 2 independent parts, one for each index of `groups`. A program takes and returns all parts, laid end to end along the dimension named above; an argument that names none is the same for every part. Nothing has to cross between parts.
Inputs may be any that keep to these rules, and one draw needn't show every extreme that they name: `roots`: entries are distinct; 0 and 7 are always among them. `inverse_store`: each slot is a dense matrix.
All inputs are finite; a program needn't handle non-finite values.
Results may differ from a plain program's by a relative error of at most 0.0051.
Values may be sent and summed in bfloat16 or wider, within the bound.
A program may use at most 64 MiB of HBM per device.

v0:
```python
import math

import jax
import jax.numpy as jnp
from jax import lax
from jax.sharding import PartitionSpec as P


def broadcast(shard, axis, root):
    mine = lax.axis_index(axis) == root
    return lax.psum(jnp.where(mine, shard, jnp.zeros_like(shard)), axis)


def per_device(embeddings, omega, phases, index_list, inverse_store, roots, residual_in):
    width = inverse_store.shape[1]
    blocks = roots.shape[0]
    scale = math.sqrt(2.0 / width)
    slot = inverse_store[0]
    residual = residual_in.astype(jnp.float32)
    results = []
    for block in range(blocks):
        cols = index_list[block * width : (block + 1) * width]
        chosen = jnp.take(omega, cols, axis=1)
        proj = jnp.dot(embeddings, chosen, preferred_element_type=jnp.float32)
        feats = (scale * jnp.cos(proj + jnp.take(phases, cols)[None, :])).astype(jnp.bfloat16)
        rounded = residual.astype(jnp.bfloat16)
        owner = roots[block]
        corr = lax.dot_general(
            feats, rounded, (((0,), (0,)), ((), ())), preferred_element_type=jnp.float32
        )
        total = lax.psum(corr, "rows").astype(jnp.bfloat16)
        local_change = jnp.dot(slot, total, preferred_element_type=jnp.float32).astype(jnp.bfloat16)
        change = broadcast(local_change, "rows", owner)
        residual = residual - jnp.dot(feats, change, preferred_element_type=jnp.float32)
        results.append(change)
    return (jnp.stack(results), residual.astype(jnp.bfloat16))


def solution(mesh):
    in_specs = (
        P(("groups", "rows"), None),
        P(),
        P(),
        P(),
        P(("groups", "rows"), None, None),
        P(),
        P(("groups", "rows"), "cls"),
    )
    out_specs = (P("groups", None, "cls"), P(("groups", "rows"), "cls"))
    return jax.shard_map(
        per_device, mesh=mesh, in_specs=in_specs, out_specs=out_specs, check_vma=False
    )
```

profile of v0, /device:TPU:0, one launch (start us, length us, event | category | flops | bytes accessed | tf_op | source)
XLA Modules:
  0.0 608.7 jit_solution(12986690645019901227)
XLA Ops:
  9.4 6.1 %gather_fusion.3 = f32[1024]{0:T(1024)S(1)} fusion(f32[3072]{0:T(1024)S(1)} %copy-done.1, s32[1024]{0:T(1024)S(1)} %get-tuple-element.18), kind=kCustom, calls=%fused_computation.4.clone | custom fusion | bytes 12288 | tf_op jit(solution)/shard_map/jit(_take)/gather | solution.py:25
  15.5 6.2 %gather_fusion.1 = f32[1024]{0:T(1024)S(1)} fusion(f32[3072]{0:T(1024)S(1)} %copy-done.1, s32[1024]{0:T(1024)S(1)} %get-tuple-element.19), kind=kCustom, calls=%fused_computation.1.clone | custom fusion | bytes 12288 | tf_op jit(solution)/shard_map/jit(_take)/gather | solution.py:25
  21.7 6.2 %gather_fusion.5 = f32[1024]{0:T(1024)S(1)} fusion(f32[3072]{0:T(1024)S(1)} %copy-done.1, s32[1024]{0:T(1024)S(1)} %get-tuple-element.20), kind=kCustom, calls=%fused_computation.5.clone | custom fusion | bytes 12288 | tf_op jit(solution)/shard_map/jit(_take)/gather | solution.py:25
  27.9 8.6 %copy.13 = bf16[1024,3072]{0,1:T(8,128)(2,1)} copy(bf16[1024,3072]{1,0:T(8,128)(2,1)} %param.12) | data formatting | bytes 12582912 | tf_op args[1]
  36.5 9.6 %gather_fusion = bf16[1024,1024]{1,0:T(8,128)(2,1)} fusion(bf16[1024,3072]{0,1:T(8,128)(2,1)} %copy.13, s32[1024]{0:T(1024)S(1)} %get-tuple-element.19), kind=kCustom, calls=%fused_computation.clone | custom fusion | bytes 4198400 | tf_op jit(solution)/shard_map/jit(_take)/gather | solution.py:23
  46.2 10.3 %multiply_convert_fusion.2 = bf16[1024,512]{1,0:T(8,128)(2,1)S(1)} fusion(bf16[512,1024]{1,0:T(8,128)(2,1)} %param.11, bf16[1024,1024]{1,0:T(8,128)(2,1)} %gather_fusion, pred[1024]{0:T(1024)(128)(4,1)S(1)} %get-tuple-element.17, f32[1024]{0:T(1024)S(1)} %get-tuple-element.16), kind=kOutput, calls=%fused_computation.24 | convolution fusion | flops 1076363264 | bytes 4199424 | tf_op jit(solution)/shard_map/dot_general | solution.py:24
  59.5 93.3 %all-reduce.12 = bf16[1024,512]{1,0:T(8,128)(2,1)S(1)} all-reduce(f32[1024,512]{1,0:T(8,128)} %fusion.69), channel_id=1, replica_groups=mesh['groups'=2,'rows'=8,'cls'=2] {'rows'}, use_global_device_ids=true, to_apply=%region_0.3 | all-reduce | flops 524288 | bytes 3145728 | tf_op jit(solution)/shard_map/psum | solution.py:31
  153.5 2.3 fusion.49
  156.1 9.6 %gather_fusion.2 = bf16[1024,1024]{1,0:T(8,128)(2,1)} fusion(bf16[1024,3072]{0,1:T(8,128)(2,1)} %copy.13, s32[1024]{0:T(1024)S(1)} %get-tuple-element.18), kind=kCustom, calls=%fused_computation.2.clone | custom fusion | bytes 4198400 | tf_op jit(solution)/shard_map/jit(_take)/gather | solution.py:23
  166.4 10.3 %multiply_convert_fusion.1 = bf16[1024,512]{1,0:T(8,128)(2,1)S(1)} fusion(bf16[512,1024]{1,0:T(8,128)(2,1)} %param.11, bf16[1024,1024]{1,0:T(8,128)(2,1)} %gather_fusion.2, pred[1024]{0:T(1024)(128)(4,1)S(1)} %get-tuple-element.9, f32[1024]{0:T(1024)S(1)} %get-tuple-element.8), kind=kOutput, calls=%fused_computation.23 | convolution fusion | flops 1076363264 | bytes 4199424 | tf_op jit(solution)/shard_map/dot_general | solution.py:24
  176.6 57.3 %all-reduce.7.cloned.1.call-done = bf16[1024,512]{0,1:T(8,128)(2,1)} async-done(((bf16[1024,512]{0,1:T(8,128)(2,1)}), bf16[1024,512]{0,1:T(8,128)(2,1)}) %all-reduce.7.cloned.1.call-update) | async-done | bytes 1048592 | tf_op jit(solution)/shard_map/psum | solution.py:11
  234.0 2.4 convolution_subtract_fusion.2
  239.5 91.4 %all-reduce.13 = bf16[1024,512]{1,0:T(8,128)(2,1)} all-reduce(f32[1024,512]{1,0:T(8,128)} %fusion.60), channel_id=1, replica_groups=mesh['groups'=2,'rows'=8,'cls'=2] {'rows'}, use_global_device_ids=true, to_apply=%region_2.5 | all-reduce | flops 524288 | bytes 3145728 | tf_op jit(solution)/shard_map/psum | solution.py:31
  330.8 3.5 fusion.43
  334.4 9.6 %gather_fusion.4 = bf16[1024,1024]{1,0:T(8,128)(2,1)} fusion(bf16[1024,3072]{0,1:T(8,128)(2,1)} %copy.13, s32[1024]{0:T(1024)S(1)} %get-tuple-element.20), kind=kCustom, calls=%fused_computation.3.clone | custom fusion | bytes 4198400 | tf_op jit(solution)/shard_map/jit(_take)/gather | solution.py:23
  344.6 10.9 %multiply_convert_fusion = bf16[1024,512]{1,0:T(8,128)(2,1)} fusion(bf16[512,1024]{1,0:T(8,128)(2,1)} %param.11, bf16[1024,1024]{1,0:T(8,128)(2,1)} %gather_fusion.4, pred[1024]{0:T(1024)(128)(4,1)S(1)} %get-tuple-element.15, f32[1024]{0:T(1024)S(1)} %get-tuple-element.14), kind=kOutput, calls=%fused_computation.22 | convolution fusion | flops 1076363264 | bytes 4199424 | tf_op jit(solution)/shard_map/dot_general | solution.py:24
  355.6 56.8 %all-reduce.9.cloned.1.call-done = bf16[1024,512]{0,1:T(8,128)(2,1)} async-done(((bf16[1024,512]{0,1:T(8,128)(2,1)}), bf16[1024,512]{0,1:T(8,128)(2,1)}) %all-reduce.9.cloned.1.call-update) | async-done | bytes 1048592 | tf_op jit(solution)/shard_map/psum | solution.py:11
  412.4 2.4 convolution_subtract_fusion.1
  417.8 91.6 %all-reduce.14 = bf16[1024,512]{1,0:T(8,128)(2,1)} all-reduce(f32[1024,512]{1,0:T(8,128)} %fusion.58), channel_id=1, replica_groups=mesh['groups'=2,'rows'=8,'cls'=2] {'rows'}, use_global_device_ids=true, to_apply=%region_4.7 | all-reduce | flops 524288 | bytes 3145728 | tf_op jit(solution)/shard_map/psum | solution.py:31
  509.4 3.6 fusion.37
  513.0 77.9 %all-reduce.11.cloned.1.call-done = bf16[1024,512]{0,1:T(8,128)(2,1)} async-done(((bf16[1024,512]{0,1:T(8,128)(2,1)}), bf16[1024,512]{0,1:T(8,128)(2,1)}) %all-reduce.11.cloned.1.call-update) | async-done | bytes 1048592 | tf_op jit(solution)/shard_map/psum | solution.py:11
  590.9 3.5 pad_maximum_fusion
  594.4 4.7 copy.16
  599.1 3.1 fusion.33
  (32 shorter events, 11.6 us)
Async XLA Ops:
  7.2 146.4 %copy-start = (bf16[1,1024,1024]{2,1,0:T(8,128)(2,1)S(1)}, bf16[1,1024,1024]{2,1,0:T(8,128)(2,1)}, u32[]{:S(2)}) copy-start(bf16[1,1024,1024]{2,1,0:T(8,128)(2,1)} %param.15) | copy-start | bytes 6291460
  7.2 2.2 copy-start.1
  7.2 226.8 %all-reduce.7.cloned.1.call-start = ((), (), s32[]{:S(2)}) async-start(), calls=%async_computation | async-start | bytes 2097152 | tf_op jit(solution)/shard_map/psum | solution.py:11
  36.5 9.6 %copy-start.9 = (s32[3072]{0:T(1024)S(1)}, s32[3072]{0:T(1024)}, u32[]{:S(2)}) copy-start(s32[3072]{0:T(1024)} %param.14) | copy-start | bytes 36868
  46.1 11.3 %copy-start.8 = (bf16[512,512]{1,0:T(8,128)(2,1)S(1)}, bf16[512,512]{1,0:T(8,128)(2,1)}, u32[]{:S(2)}) copy-start(bf16[512,512]{1,0:T(8,128)(2,1)} %param.17) | copy-start | bytes 1572868
  56.4 1.0 copy-start.6
  155.9 256.5 %all-reduce.9.cloned.1.call-start = ((), (), s32[]{:S(2)}) async-start(), calls=%async_computation.1 | async-start | bytes 2097152 | tf_op jit(solution)/shard_map/psum | solution.py:11
  236.4 1.0 copy-start.3
  334.3 256.5 %all-reduce.11.cloned.1.call-start = ((), (), s32[]{:S(2)}) async-start(), calls=%async_computation.2 | async-start | bytes 2097152 | tf_op jit(solution)/shard_map/psum | solution.py:11
  412.4 3.4 copy-start.7
  414.7 1.0 copy-start.4
  509.4 81.5 %copy-start.2 = (bf16[1024,512]{0,1:T(8,128)(2,1)S(1)}, bf16[1024,512]{0,1:T(8,128)(2,1)}, u32[]{:S(2)}) copy-start(bf16[1024,512]{0,1:T(8,128)(2,1)} %all-reduce.9.cloned.1.call-done) | copy-start | bytes 3145732
  594.4 4.7 copy-start.5
Sparse Core Ops, SparseCore 0:
  156.0 77.9 all-reduce.6
  334.5 77.8 all-reduce.8
  513.1 77.7 all-reduce.10
where the time goes:
time: 610 us; the launch traced here: 609 us
  blocking collectives  276 us (45%)
  waiting for transfers between devices  192 us (31%)
  local copies, waits for them, and re-layouts  65.1 us (11%)
  matrix products  54.9 us (9%)
  between operations  15.9 us (3%)
    psum x3, blocking collectives, per_device(): total = lax.psum(corr, 'rows').astype(jnp.bfloat16)  276 us
    psum x3, waiting for transfers between devices, broadcast(): return lax.psum(jnp.where(mine, shard, jnp.zeros_like(shard)), axis)  192 us
    dot_general x3, matrix products, per_device(): proj = jnp.dot(embeddings, chosen, preferred_element_type=jnp.float32)  31.5 us
    gather x3, local copies, waits for them, and re-layouts, per_device(): chosen = jnp.take(omega, cols, axis=1)  28.8 us
    gather x3, local copies, waits for them, and re-layouts, per_device(): jnp.take(phases, cols)[None, :]  18.5 us
    unnamed x22, local copies, waits for them, and re-layouts  16.4 us
  transfers between devices with their start and end apart: 3, of which 3 were waited for; matrix products, arithmetic and copies ran while one was open for 7% of the time, Pallas kernels for 0%

commit v1 on v0

v1 whole, which is shorter than its diff:
```python
import functools
import math

import jax
import jax.numpy as jnp
import numpy as np
from jax import lax
from jax.experimental import pallas as pl
from jax.experimental.pallas import tpu as pltpu
from jax.sharding import PartitionSpec as P

MESH = pl.DeviceIdType.MESH
F32 = jnp.float32
BF16 = jnp.bfloat16


def cos_coefficients(degree):
    top = math.pi**2 * 1.0001
    cheb = np.polynomial.chebyshev.Chebyshev.interpolate(
        lambda u: np.cos(np.sqrt(np.maximum(u, 0.0))), degree, domain=[0.0, top]
    )
    return [float(c) for c in cheb.convert(kind=np.polynomial.Polynomial).coef]


COS = cos_coefficients(7)
TWO_PI_HI = 6.28125
TWO_PI_LO = 2.0 * math.pi - TWO_PI_HI


def cosine(x):
    turns = jnp.round(x * (1.0 / (2.0 * math.pi)))
    r = (x - turns * TWO_PI_HI) - turns * TWO_PI_LO
    u = r * r
    y = jnp.full_like(u, COS[-1])
    for c in COS[-2::-1]:
        y = y * u + c
    return y


def tile_of(size, want):
    return want if size % want == 0 else size


def body(
    n, inner, roots_ref, emb_ref, omega_ref, phases_ref, index_ref, slot_ref, res_in_ref,
    changes_ref, res_ref,
    plain, feats, resid, corr, ybuf, zout, zbuf, chg, abuf, inv,
    a_sem, ys_sem, zs_sem, cz_sem, cy_sem, iz_sem, iy_sem, ic_sem, loc_sem, out_sem,
):
    outer = n // inner
    me = lax.axis_index("rows")
    core = lax.axis_index("cls")
    mi = lax.rem(me, inner)
    mo = lax.div(me, inner)
    partner = mo * inner + (inner - 1 - mi)
    rows, din = emb_ref.shape
    pool = omega_ref.shape[1]
    blocks, width = chg.shape[0], chg.shape[3]
    classes = resid.shape[1]
    share = classes // n
    pending = []

    def send(src, dst, sems, device):
        copy = pltpu.make_async_remote_copy(
            src_ref=src, dst_ref=dst, send_sem=sems[0], recv_sem=sems[1],
            device_id=device, device_id_type=MESH,
        )
        copy.start()
        pending.append(copy)
        return copy

    def arrived(dst, sems):
        pltpu.make_async_remote_copy(
            src_ref=dst, dst_ref=dst, send_sem=sems[0], recv_sem=sems[1],
            device_id={"rows": partner}, device_id_type=MESH,
        ).wait_recv()

    def at(sem, *idx):
        return sem.at[(0, *idx)], sem.at[(1, *idx)]

    def other(d):
        return lax.rem(mo + d, outer)

    barrier = pltpu.get_barrier_semaphore()
    for d in range(1, n):
        pl.semaphore_signal(
            barrier, inc=1, device_id={"rows": lax.rem(me + d, n)}, device_id_type=MESH
        )
    pl.semaphore_signal(barrier, inc=1, device_id={"cls": 1 - core}, device_id_type=MESH)
    pl.semaphore_wait(barrier, n)

    for d in range(1, n):
        to = lax.rem(me + d, n)
        send(slot_ref.at[core, to], abuf.at[me], at(a_sem, d), {"rows": to})
    own = pltpu.make_async_copy(slot_ref.at[core, me], abuf.at[me], loc_sem.at[0])
    own.start()
    res_load = pltpu.make_async_copy(res_in_ref, res_ref, loc_sem.at[1])
    res_load.start()

    scale = math.sqrt(2.0 / width)
    wide = tile_of(pool, 512)

    @pl.loop(0, pool // wide)
    def _(t):
        cols = pl.ds(pl.multiple_of(t * wide, wide), wide)
        proj = jnp.dot(emb_ref[...], omega_ref[:, cols], preferred_element_type=F32)
        plain[:, cols] = (scale * cosine(proj + phases_ref[:, cols])).astype(BF16)

    narrow = tile_of(pool, 256)

    @pl.loop(0, pool // narrow)
    def _(t):
        cols = pl.ds(pl.multiple_of(t * narrow, narrow), narrow)
        line = lax.broadcasted_iota(jnp.int32, (pool, narrow), 0)
        pick = jnp.where(line == index_ref[:, cols], 1.0, 0.0).astype(BF16)
        feats[:, cols] = jnp.dot(plain[...], pick, preferred_element_type=F32).astype(BF16)

    res_load.wait()
    resid[...] = res_ref[...].astype(F32)

    step = tile_of(width, 256)

    def correlate(b):
        rounded = resid[...].astype(BF16)

        @pl.loop(0, width // step)
        def _(t):
            here = pl.multiple_of(t * step, step)
            part = lax.dot_general(
                rounded, feats[:, pl.ds(b * width + here, step)],
                (((0,), (0,)), ((), ())), preferred_element_type=F32,
            )
            corr[b, :, :, pl.ds(here, step)] = part.astype(BF16).reshape(n, share, step)

        for d in range(1, outer + 1):
            o = other(d)
            send(
                corr.at[b, o * inner + (inner - 1 - mi)], ybuf.at[b, o],
                at(ys_sem, b, d % outer), {"rows": partner},
            )

    def pair_sum(b, d):
        o = other(d)
        arrived(ybuf.at[b, o], at(ys_sem, b, d % outer))
        return corr[b, o * inner + mi].astype(F32) + ybuf[b, o].astype(F32)

    def scatter(b):
        for d in range(1, outer):
            o = other(d)
            zout[b, d] = pair_sum(b, d).astype(BF16)
            send(zout.at[b, d], zbuf.at[b, d], at(zs_sem, b, d), {"rows": o * inner + mi})

    def total(b):
        acc = pair_sum(b, 0)
        for d in range(1, outer):
            arrived(zbuf.at[b, d], at(zs_sem, b, d))
            acc = acc + zbuf[b, d].astype(F32)
        return acc.astype(BF16)

    def gather_first(ref, z_sem, y_sem, b):
        for d in range(1, outer):
            send(ref.at[me], ref.at[me], at(z_sem, b, d), {"rows": other(d) * inner + mi})
        send(ref.at[me], ref.at[me], at(y_sem, b, 0), {"rows": partner})

    def gather_second(ref, z_sem, y_sem, b):
        for d in range(1, outer):
            src = lax.rem(mo - d + outer, outer) * inner + mi
            arrived(ref.at[src], at(z_sem, b, d))
            send(ref.at[src], ref.at[src], at(y_sem, b, d), {"rows": partner})

    def gather_third(ref, y_sem, b):
        for d in range(outer):
            src = lax.rem(mo - d + outer, outer) * inner + (inner - 1 - mi)
            arrived(ref.at[src], at(y_sem, b, d))

    def inv_first(b):
        gather_first(inv.at[b, core], iz_sem, iy_sem, b)

    def inv_second(b):
        gather_second(inv.at[b, core], iz_sem, iy_sem, b)

    def inv_third(b):
        gather_third(inv.at[b, core], iy_sem, b)
        send(inv.at[b, core], inv.at[b, core], at(ic_sem, b), {"cls": 1 - core})

    def inv_wait(b):
        arrived(inv.at[b, 1 - core], at(ic_sem, b))

    def solve(b):
        piece = total(b)
        inv_wait(b)
        half = width // 2
        for c in range(2):
            out = lax.dot_general(
                piece, inv[b, c].reshape(half, width),
                (((1,), (1,)), ((), ())), preferred_element_type=F32,
            )
            chg[b, me, :, c * half : (c + 1) * half] = out.astype(BF16)
        gather_first(chg.at[b], cz_sem, cy_sem, b)

    def update(b):
        gather_third(chg.at[b], cy_sem, b)
        save = pltpu.make_async_copy(chg.at[b], changes_ref.at[b], out_sem.at[b])
        save.start()
        change = chg[b].reshape(classes, width)
        high = tile_of(rows, 256)

        @pl.loop(0, rows // high)
        def _(t):
            here = pl.ds(pl.multiple_of(t * high, high), high)
            resid[here, :] = resid[here, :] - lax.dot_general(
                feats[here, b * width : (b + 1) * width], change,
                (((1,), (1,)), ((), ())), preferred_element_type=F32,
            )

        return save

    correlate(0)
    for d in range(1, n):
        arrived(abuf.at[lax.rem(me - d + n, n)], at(a_sem, d))
    own.wait()
    for b in range(blocks):
        inv[b, core, me] = abuf[roots_ref[b]]
    inv_first(0)
    scatter(0)
    inv_second(0)
    saves = []
    for b in range(blocks):
        if b + 1 < blocks:
            inv_first(b + 1)
        if b == 0:
            inv_third(0)
        solve(b)
        if b + 1 < blocks:
            inv_second(b + 1)
        gather_second(chg.at[b], cz_sem, cy_sem, b)
        saves.append(update(b))
        if b + 1 < blocks:
            correlate(b + 1)
            inv_third(b + 1)
            scatter(b + 1)
    res_ref[...] = resid[...].astype(BF16)
    for save in saves:
        save.wait()
    for copy in pending:
        copy.wait_send()


def per_device(n, embeddings, omega, phases, index_list, inverse_store, roots, residual_in):
    rows, din = embeddings.shape
    pool = omega.shape[1]
    width = inverse_store.shape[1]
    blocks = roots.shape[0]
    classes = residual_in.shape[1]
    inner = 2
    outer = n // inner
    share = classes // n
    part = width // (2 * n)
    vmem = pl.BlockSpec(memory_space=pltpu.VMEM)
    anywhere = pl.BlockSpec(memory_space=pl.ANY)
    dma = pltpu.SemaphoreType.DMA
    flops = 2 * rows * pool * (din + pool + 2 * classes)
    changes, residual = pl.pallas_call(
        functools.partial(body, n, inner),
        out_shape=(
            jax.ShapeDtypeStruct((blocks, n, share, width), BF16),
            jax.ShapeDtypeStruct((rows, classes), BF16),
        ),
        in_specs=[pl.BlockSpec(memory_space=pltpu.SMEM), vmem, vmem, vmem, vmem, anywhere, anywhere],
        out_specs=(anywhere, vmem),
        scratch_shapes=[
            pltpu.VMEM((rows, pool), BF16),
            pltpu.VMEM((rows, pool), BF16),
            pltpu.VMEM((rows, classes), F32),
            pltpu.VMEM((blocks, n, share, width), BF16),
            pltpu.VMEM((blocks, outer, share, width), BF16),
            pltpu.VMEM((blocks, outer, share, width), BF16),
            pltpu.VMEM((blocks, outer, share, width), BF16),
            pltpu.VMEM((blocks, n, share, width), BF16),
            pltpu.VMEM((n, part, width), BF16),
            pltpu.VMEM((blocks, 2, n, part, width), BF16),
            dma((2, n)),
            dma((2, blocks, outer)),
            dma((2, blocks, outer)),
            dma((2, blocks, outer)),
            dma((2, blocks, outer)),
            dma((2, blocks, outer)),
            dma((2, blocks, outer)),
            dma((2, blocks)),
            dma((2,)),
            dma((blocks,)),
        ],
        compiler_params=pltpu.CompilerParams(
            collective_id=0, has_side_effects=True, vmem_limit_bytes=56 * 1024 * 1024
        ),
        cost_estimate=pl.CostEstimate(
            flops=flops, bytes_accessed=20 * 1024 * 1024, transcendentals=rows * pool
        ),
    )(
        roots, embeddings, omega, phases[None, :], index_list[None, :],
        inverse_store[0].reshape(2, n, part, width), residual_in,
    )
    changes = jnp.swapaxes(changes.reshape(blocks, classes, width), 1, 2)
    return changes, residual


def solution(mesh):
    in_specs = (
        P(("groups", "rows"), None),
        P(),
        P(),
        P(),
        P(("groups", "rows"), None, None),
        P(),
        P(("groups", "rows"), "cls"),
    )
    out_specs = (P("groups", None, "cls"), P(("groups", "rows"), "cls"))
    return jax.shard_map(
        functools.partial(per_device, mesh.shape["rows"]),
        mesh=mesh, in_specs=in_specs, out_specs=out_specs, check_vma=False,
    )
```

time: 610 us -> 183 us (0.30)
  blocking collectives: 276 us -> 0 us
  waiting for transfers between devices: 192 us -> 0 us
  Pallas kernels: 0 us -> 177 us
  local copies, waits for them, and re-layouts: 65.1 us -> 5.49 us
  matrix products: 54.9 us -> 0 us
  between operations: 15.9 us -> 0.65 us
    psum x3 -> x0, blocking collectives: 276 us -> none  [per_device(): total = lax.psum(corr, 'rows').astype(jnp.bfloat16)]
    psum x3 -> x0, waiting for transfers between devices: 192 us -> none  [broadcast(): return lax.psum(jnp.where(mine, shard, jnp.zeros_like(shard)), axis)]
    pallas_call x0 -> x1, Pallas kernels: none -> 177 us  [per_device(): pl.pallas_call(functools.partial(body, n, inner), out_shape=(jax.ShapeDty...]
    dot_general x12 -> x0, matrix products: 54.9 us -> none  [the longest x3 31.5 us: per_device(): proj = jnp.dot(embeddings, chosen, preferred_element_type=jnp.float32)]
    gather x6 -> x0, local copies, waits for them, and re-layouts: 47.3 us -> none  [the longest x3 28.8 us: per_device(): chosen = jnp.take(omega, cols, axis=1)]
    unnamed x22 -> x3, local copies, waits for them, and re-layouts: 16.4 us -> 0.8 us
  transfers between devices with their start and end apart: 3 -> 0, of which waited for: 3 -> 0; matrix products, arithmetic and copies ran while one was open for 7% -> 0% of each run, Pallas kernels for 0% -> 0%
where the time goes in v1:
time: 183 us
  Pallas kernels  177 us (97%)
  local copies, waits for them, and re-layouts  5.49 us (3%)
    pallas_call x1, Pallas kernels, per_device(): pl.pallas_call(functools.partial(body, n, inner), out_shape=(jax.ShapeDty...  177 us
    reshape x1, local copies, waits for them, and re-layouts, per_device(): changes = jnp.swapaxes(changes.reshape(blocks, classes, width), 1, 2)  4.69 us

profile of v1, /device:TPU:0, one launch (start us, length us, event | category | flops | bytes accessed | tf_op | source)
XLA Modules:
  0.0 182.9 jit_solution(11449383760161361769)
XLA Ops:
  0.6 176.7 %shard_map.86 = (bf16[3,8,64,1024]{3,2,1,0:T(8,128)(2,1)}, bf16[512,512]{1,0:T(8,128)(2,1)}) custom-call(s32[3]{0:T(128)} %roots_ref.1, bf16[512,1024]{1,0:T(8,128)(2,1)} %emb_ref.1, bf16[1024,3072]{1,0:T(8,128)(2,1)} %omega_ref.1, f32[1,3072]{1,0:T(1,128)} %bitcast.8, s32[1,3072]{1,0:T(1,128)} %bitcast.9, bf16[2,8,64,1024]{3,2,1,0:T(8,128)(2,1)} %bitcast.7, ...), custom_call_target="tpu_custom_call" | custom-call | flops 16106127360 | bytes 20971520 | tf_op jit(solution)/shard_map/pallas_call | solution.py:263
  177.4 0.0 copy-start
  177.4 4.7 %copy.9 = bf16[3,512,1024]{1,2,0:T(8,128)(2,1)} copy(bf16[3,512,1024]{2,1,0:T(8,128)(2,1)} %bitcast.6) | data formatting | bytes 6291456 | tf_op jit(solution)/shard_map/reshape | solution.py:303
  182.1 0.0 copy-done
  182.1 0.8 copy.11
Async XLA Ops:
  177.4 4.7 %copy-start = (bf16[512,512]{1,0:T(8,128)(2,1)S(1)}, bf16[512,512]{1,0:T(8,128)(2,1)}, u32[]{:S(2)}) copy-start(bf16[512,512]{1,0:T(8,128)(2,1)} %get-tuple-element.9) | copy-start | bytes 1572868

commit v2 on v1

v2 whole, which is shorter than its diff:
```python
import functools
import math

import jax
import jax.numpy as jnp
import numpy as np
from jax import lax
from jax.experimental import pallas as pl
from jax.experimental.pallas import tpu as pltpu
from jax.sharding import PartitionSpec as P

MESH = pl.DeviceIdType.MESH
F32 = jnp.float32
BF16 = jnp.bfloat16


def cos_coefficients(degree):
    top = math.pi**2 * 1.0001
    cheb = np.polynomial.chebyshev.Chebyshev.interpolate(
        lambda u: np.cos(np.sqrt(np.maximum(u, 0.0))), degree, domain=[0.0, top]
    )
    return [float(c) for c in cheb.convert(kind=np.polynomial.Polynomial).coef]


COS = cos_coefficients(7)
TWO_PI_HI = 6.28125
TWO_PI_LO = 2.0 * math.pi - TWO_PI_HI


def cosine(x):
    turns = jnp.round(x * (1.0 / (2.0 * math.pi)))
    r = (x - turns * TWO_PI_HI) - turns * TWO_PI_LO
    u = r * r
    y = jnp.full_like(u, COS[-1])
    for c in COS[-2::-1]:
        y = y * u + c
    return y


def tile_of(size, want):
    return want if size % want == 0 else size


def body(
    n, inner, blocks, halves, roots_ref, emb_ref, omega_ref, phases_ref, index_ref, slot_ref, res_in_ref,
    changes_ref, res_ref,
    plain, feats, resid, corr, ybuf, zout, zbuf, pair, chg, abuf, inv,
    a_sem, ys_sem, zs_sem, p_sem, cz_sem, cy_sem, iz_sem, ic_sem, loc_sem, out_sem,
):
    outer = n // inner
    me = lax.axis_index("rows")
    core = lax.axis_index("cls")
    mi = lax.rem(me, inner)
    mo = lax.div(me, inner)
    partner = mo * inner + (inner - 1 - mi)
    rows, din = emb_ref.shape
    pool = omega_ref.shape[1]
    width = corr.shape[3]
    lines = resid.shape[1] // halves
    share = lines // n
    fold = width // inner
    pending = []

    def send(src, dst, sems, device):
        copy = pltpu.make_async_remote_copy(
            src_ref=src, dst_ref=dst, send_sem=sems[0], recv_sem=sems[1],
            device_id=device, device_id_type=MESH,
        )
        copy.start()
        pending.append(copy)
        return copy

    def arrived(dst, sems):
        pltpu.make_async_remote_copy(
            src_ref=dst, dst_ref=dst, send_sem=sems[0], recv_sem=sems[1],
            device_id={"rows": partner}, device_id_type=MESH,
        ).wait_recv()

    def at(sem, *idx):
        return sem.at[(0, *idx)], sem.at[(1, *idx)]

    def other(d):
        return lax.rem(mo + d, outer)

    barrier = pltpu.get_barrier_semaphore()
    for d in range(1, n):
        pl.semaphore_signal(
            barrier, inc=1, device_id={"rows": lax.rem(me + d, n)}, device_id_type=MESH
        )
    pl.semaphore_signal(barrier, inc=1, device_id={"cls": 1 - core}, device_id_type=MESH)
    pl.semaphore_wait(barrier, n)

    for d in range(1, n):
        to = lax.rem(me + d, n)
        send(
            slot_ref.at[lax.rem(to, inner), core, lax.div(to, inner)], abuf.at[me],
            at(a_sem, d), {"rows": to},
        )
    own = pltpu.make_async_copy(slot_ref.at[mi, core, mo], abuf.at[me], loc_sem.at[0])
    own.start()
    res_load = pltpu.make_async_copy(res_in_ref, res_ref, loc_sem.at[1])
    res_load.start()

    scale = math.sqrt(2.0 / width)
    wide = tile_of(pool, 512)

    @pl.loop(0, pool // wide)
    def _(t):
        cols = pl.ds(pl.multiple_of(t * wide, wide), wide)
        proj = jnp.dot(emb_ref[...], omega_ref[:, cols], preferred_element_type=F32)
        plain[:, cols] = (scale * cosine(proj + phases_ref[:, cols])).astype(BF16)

    narrow = tile_of(pool, 256)

    @pl.loop(0, pool // narrow)
    def _(t):
        cols = pl.ds(pl.multiple_of(t * narrow, narrow), narrow)
        line = lax.broadcasted_iota(jnp.int32, (pool, narrow), 0)
        pick = jnp.where(line == index_ref[:, cols], 1.0, 0.0).astype(BF16)
        feats[:, cols] = jnp.dot(plain[...], pick, preferred_element_type=F32).astype(BF16)

    res_load.wait()
    resid[...] = res_ref[...].astype(F32)

    step = tile_of(width, 256)

    def correlate(b, h):
        k = b * halves + h
        rounded = resid[:, h * lines : (h + 1) * lines].astype(BF16)

        @pl.loop(0, width // step)
        def _(t):
            here = pl.multiple_of(t * step, step)
            part = lax.dot_general(
                rounded, feats[:, pl.ds(b * width + here, step)],
                (((0,), (0,)), ((), ())), preferred_element_type=F32,
            )
            corr[k, :, :, pl.ds(here, step)] = part.astype(BF16).reshape(n, share, step)

        for d in range(1, outer + 1):
            o = other(d)
            send(
                corr.at[k, o * inner + (inner - 1 - mi)], ybuf.at[k, o],
                at(ys_sem, k, d % outer), {"rows": partner},
            )

    def pair_sum(k, d):
        o = other(d)
        arrived(ybuf.at[k, o], at(ys_sem, k, d % outer))
        return corr[k, o * inner + mi].astype(F32) + ybuf[k, o].astype(F32)

    def scatter(k):
        for d in range(1, outer):
            o = other(d)
            zout[k, d] = pair_sum(k, d).astype(BF16)
            send(zout.at[k, d], zbuf.at[k, d], at(zs_sem, k, d), {"rows": o * inner + mi})

    def total(k):
        acc = pair_sum(k, 0)
        for d in range(1, outer):
            arrived(zbuf.at[k, d], at(zs_sem, k, d))
            acc = acc + zbuf[k, d].astype(F32)
        pair[k, mi] = acc.astype(BF16)
        send(pair.at[k, mi], pair.at[k, mi], at(p_sem, k), {"rows": partner})

    def inv_spread(b):
        for d in range(1, outer):
            send(
                inv.at[b, core, mo], inv.at[b, core, mo], at(iz_sem, b, d),
                {"rows": other(d) * inner + mi},
            )

    def inv_share(b):
        for d in range(1, outer):
            arrived(inv.at[b, core, lax.rem(mo - d + outer, outer)], at(iz_sem, b, d))
        send(inv.at[b, core], inv.at[b, core], at(ic_sem, b), {"cls": 1 - core})

    def inv_wait(b):
        arrived(inv.at[b, 1 - core], at(ic_sem, b))

    def solve(b, h):
        k = b * halves + h
        arrived(pair.at[k, inner - 1 - mi], at(p_sem, k))
        both = pair[k].reshape(inner * share, width)
        out = lax.dot_general(
            both, inv[b].reshape(fold, width),
            (((1,), (1,)), ((), ())), preferred_element_type=F32,
        )
        chg[k, mi, mo] = out.astype(BF16)
        mine = chg.at[k, mi, mo]
        for d in range(1, outer):
            send(mine, mine, at(cz_sem, k, d), {"rows": other(d) * inner + mi})
        send(mine, mine, at(cy_sem, k, 0), {"rows": partner})

    def forward(k):
        for d in range(1, outer):
            block = chg.at[k, mi, lax.rem(mo - d + outer, outer)]
            arrived(block, at(cz_sem, k, d))
            send(block, block, at(cy_sem, k, d), {"rows": partner})

    saves = []

    def update(b, h):
        k = b * halves + h
        for d in range(outer):
            arrived(chg.at[k, inner - 1 - mi, lax.rem(mo - d + outer, outer)], at(cy_sem, k, d))
        save = pltpu.make_async_copy(chg.at[k], changes_ref.at[k], out_sem.at[k])
        save.start()
        saves.append(save)
        high = tile_of(rows, 256)

        @pl.loop(0, rows // high)
        def _(t):
            here = pl.ds(pl.multiple_of(t * high, high), high)
            there = slice(h * lines, (h + 1) * lines)
            drop = jnp.zeros((high, lines), F32)
            for i in range(inner):
                first = b * width + i * fold
                drop = drop + lax.dot_general(
                    feats[here, first : first + fold], chg[k, i].reshape(lines, fold),
                    (((1,), (1,)), ((), ())), preferred_element_type=F32,
                )
            resid[here, there] = resid[here, there] - drop

    every = range(halves)
    for h in every:
        correlate(0, h)
    for d in range(1, n):
        arrived(abuf.at[lax.rem(me - d + n, n)], at(a_sem, d))
    own.wait()
    for b in range(blocks):
        inv[b, core, mo] = abuf[roots_ref[b]]
    inv_spread(0)
    for b in range(blocks):
        more = b + 1 < blocks
        for h in every:
            scatter(b * halves + h)
        if b == 0:
            inv_share(0)
        for h in every:
            total(b * halves + h)
        inv_wait(b)
        for h in every:
            solve(b, h)
        if more:
            inv_spread(b + 1)
        for h in every:
            forward(b * halves + h)
        for h in every:
            update(b, h)
            if more:
                correlate(b + 1, h)
                if h == 0:
                    inv_share(b + 1)
    res_ref[...] = resid[...].astype(BF16)
    for save in saves:
        save.wait()
    for copy in pending:
        copy.wait_send()


def per_device(n, embeddings, omega, phases, index_list, inverse_store, roots, residual_in):
    rows, din = embeddings.shape
    pool = omega.shape[1]
    width = inverse_store.shape[1]
    blocks = roots.shape[0]
    classes = residual_in.shape[1]
    inner = 2
    outer = n // inner
    halves = 2 if classes % (2 * n * 16) == 0 else 1
    count = blocks * halves
    lines = classes // halves
    share = lines // n
    part = width // (2 * n)
    fold = width // inner
    vmem = pl.BlockSpec(memory_space=pltpu.VMEM)
    anywhere = pl.BlockSpec(memory_space=pl.ANY)
    dma = pltpu.SemaphoreType.DMA
    flops = 2 * rows * pool * (din + pool + 2 * classes)
    changes, residual = pl.pallas_call(
        functools.partial(body, n, inner, blocks, halves),
        out_shape=(
            jax.ShapeDtypeStruct((count, inner, outer, inner * share, fold), BF16),
            jax.ShapeDtypeStruct((rows, classes), BF16),
        ),
        in_specs=[pl.BlockSpec(memory_space=pltpu.SMEM), vmem, vmem, vmem, vmem, anywhere, anywhere],
        out_specs=(anywhere, vmem),
        scratch_shapes=[
            pltpu.VMEM((rows, pool), BF16),
            pltpu.VMEM((rows, pool), BF16),
            pltpu.VMEM((rows, classes), F32),
            pltpu.VMEM((count, n, share, width), BF16),
            pltpu.VMEM((count, outer, share, width), BF16),
            pltpu.VMEM((count, outer, share, width), BF16),
            pltpu.VMEM((count, outer, share, width), BF16),
            pltpu.VMEM((count, inner, share, width), BF16),
            pltpu.VMEM((count, inner, outer, inner * share, fold), BF16),
            pltpu.VMEM((n, part, width), BF16),
            pltpu.VMEM((blocks, 2, outer, part, width), BF16),
            dma((2, n)),
            dma((2, count, outer)),
            dma((2, count, outer)),
            dma((2, count)),
            dma((2, count, outer)),
            dma((2, count, outer)),
            dma((2, blocks, outer)),
            dma((2, blocks)),
            dma((2,)),
            dma((count,)),
        ],
        compiler_params=pltpu.CompilerParams(
            collective_id=0, has_side_effects=True, vmem_limit_bytes=56 * 1024 * 1024
        ),
        cost_estimate=pl.CostEstimate(
            flops=flops, bytes_accessed=20 * 1024 * 1024, transcendentals=rows * pool
        ),
    )(
        roots, embeddings, omega, phases[None, :], index_list[None, :],
        inverse_store[0].reshape(inner, 2, outer, part, width), residual_in,
    )
    changes = changes.reshape(blocks, halves, inner, lines, fold).transpose(0, 2, 4, 1, 3)
    changes = changes.reshape(blocks, width, classes)
    return changes, residual


def solution(mesh):
    in_specs = (
        P(("groups", "rows"), None),
        P(),
        P(),
        P(),
        P(("groups", "rows"), None, None),
        P(),
        P(("groups", "rows"), "cls"),
    )
    out_specs = (P("groups", None, "cls"), P(("groups", "rows"), "cls"))
    return jax.shard_map(
        functools.partial(per_device, mesh.shape["rows"]),
        mesh=mesh, in_specs=in_specs, out_specs=out_specs, check_vma=False,
    )
```

time: 183 us -> 165 us (0.902)
  Pallas kernels: 177 us -> 152 us
  local copies, waits for them, and re-layouts: 5.49 us -> 12.9 us
    pallas_call x1, Pallas kernels: 177 us -> 152 us  [per_device(): pl.pallas_call(functools.partial(body, n, inner, blocks, halves), out_sha...]
    transpose x0 -> x1, local copies, waits for them, and re-layouts: none -> 7.28 us  [per_device(): changes.reshape(blocks, halves, inner, lines, fold).transpose(0, 2, 4, 1, 3)]
where the time goes in v2:
time: 165 us
  Pallas kernels  152 us (92%)
  local copies, waits for them, and re-layouts  12.9 us (8%)
    pallas_call x1, Pallas kernels, per_device(): pl.pallas_call(functools.partial(body, n, inner, blocks, halves), out_sha...  152 us
    transpose x1, local copies, waits for them, and re-layouts, per_device(): changes.reshape(blocks, halves, inner, lines, fold).transpose(0, 2, 4, 1, 3)  7.28 us
    reshape x1, local copies, waits for them, and re-layouts, per_device(): changes = changes.reshape(blocks, width, classes)  3.74 us

profile of v2, /device:TPU:0, one launch (start us, length us, event | category | flops | bytes accessed | tf_op | source)
XLA Modules:
  0.0 165.2 jit_solution(13635038061013774267)
XLA Ops:
  0.6 151.6 %shard_map.86 = (bf16[6,2,4,64,512]{4,3,2,1,0:T(8,128)(2,1)}, bf16[512,512]{1,0:T(8,128)(2,1)}) custom-call(s32[3]{0:T(128)} %roots_ref.1, bf16[512,1024]{1,0:T(8,128)(2,1)} %emb_ref.1, bf16[1024,3072]{1,0:T(8,128)(2,1)} %omega_ref.1, f32[1,3072]{1,0:T(1,128)} %bitcast.8, s32[1,3072]{1,0:T(1,128)} %bitcast.9, bf16[2,2,4,64,1024]{4,3,2,1,0:T(8,128)(2,1)} %bitcast.7, ...), custom_call_target="tpu_custom_call" | custom-call | flops 16106127360 | bytes 20971520 | tf_op jit(solution)/shard_map/pallas_call | solution.py:280
  152.3 7.3 %copy.9 = bf16[3,2,512,2,256]{4,3,2,1,0:T(2,128)(2,1)S(1)} copy(bf16[3,2,512,2,256]{2,4,1,3,0:T(8,128)(2,1)} %bitcast.6) | data formatting | bytes 6291456 | tf_op jit(solution)/shard_map/transpose | solution.py:321
  159.6 3.7 %reshape.11 = bf16[3,1024,512]{2,1,0:T(8,128)(2,1)} reshape(bf16[3,2,512,2,256]{4,3,2,1,0:T(2,128)(2,1)S(1)} %copy.9) | data formatting | bytes 6291456 | tf_op jit(solution)/shard_map/reshape | solution.py:322
  163.3 1.9 %copy.11 = bf16[512,512]{1,0:T(8,128)(2,1)} copy(bf16[512,512]{1,0:T(8,128)(2,1)} %get-tuple-element.9) | data formatting | bytes 1048576

commit v3 on v2

--- a/solution.py
+++ b/solution.py
@@ -150,28 +150,28 @@
         return corr[k, o * inner + mi].astype(F32) + ybuf[k, o].astype(F32)
 
     def scatter(k):
-        for d in range(1, outer):
+        for d in sorted(range(1, outer), key=lambda d: abs(2 * d - outer)):
             o = other(d)
             zout[k, d] = pair_sum(k, d).astype(BF16)
             send(zout.at[k, d], zbuf.at[k, d], at(zs_sem, k, d), {"rows": o * inner + mi})
 
     def total(k):
         acc = pair_sum(k, 0)
-        for d in range(1, outer):
+        for d in sorted(range(1, outer), key=lambda d: abs(2 * d - outer)):
             arrived(zbuf.at[k, d], at(zs_sem, k, d))
             acc = acc + zbuf[k, d].astype(F32)
         pair[k, mi] = acc.astype(BF16)
         send(pair.at[k, mi], pair.at[k, mi], at(p_sem, k), {"rows": partner})
 
     def inv_spread(b):
-        for d in range(1, outer):
+        for d in sorted(range(1, outer), key=lambda d: abs(2 * d - outer)):
             send(
                 inv.at[b, core, mo], inv.at[b, core, mo], at(iz_sem, b, d),
                 {"rows": other(d) * inner + mi},
             )
 
     def inv_share(b):
-        for d in range(1, outer):
+        for d in sorted(range(1, outer), key=lambda d: abs(2 * d - outer)):
             arrived(inv.at[b, core, lax.rem(mo - d + outer, outer)], at(iz_sem, b, d))
         send(inv.at[b, core], inv.at[b, core], at(ic_sem, b), {"cls": 1 - core})
 
@@ -188,12 +188,12 @@
         )
         chg[k, mi, mo] = out.astype(BF16)
         mine = chg.at[k, mi, mo]
-        for d in range(1, outer):
+        for d in sorted(range(1, outer), key=lambda d: abs(2 * d - outer)):
             send(mine, mine, at(cz_sem, k, d), {"rows": other(d) * inner + mi})
         send(mine, mine, at(cy_sem, k, 0), {"rows": partner})
 
     def forward(k):
-        for d in range(1, outer):
+        for d in sorted(range(1, outer), key=lambda d: abs(2 * d - outer)):
             block = chg.at[k, mi, lax.rem(mo - d + outer, outer)]
             arrived(block, at(cz_sem, k, d))
             send(block, block, at(cy_sem, k, d), {"rows": partner})
@@ -239,8 +239,8 @@
             inv_share(0)
         for h in every:
             total(b * halves + h)
-        inv_wait(b)
-        for h in every:
+            if h == 0:
+                inv_wait(b)
             solve(b, h)
         if more:
             inv_spread(b + 1)

time: 165 us -> 161 us (0.976)
  Pallas kernels: 152 us -> 147 us
    pallas_call x1, Pallas kernels: 152 us -> 147 us  [per_device(): pl.pallas_call(functools.partial(body, n, inner, blocks, halves), out_sha...]
where the time goes in v3:
time: 161 us; the launch traced here: 160 us
  Pallas kernels  147 us (91%)
  local copies, waits for them, and re-layouts  12.9 us (8%)
    pallas_call x1, Pallas kernels, per_device(): pl.pallas_call(functools.partial(body, n, inner, blocks, halves), out_sha...  147 us
    transpose x1, local copies, waits for them, and re-layouts, per_device(): changes.reshape(blocks, halves, inner, lines, fold).transpose(0, 2, 4, 1, 3)  7.28 us
    reshape x1, local copies, waits for them, and re-layouts, per_device(): changes = changes.reshape(blocks, width, classes)  3.74 us

profile of v3, /device:TPU:0, one launch (start us, length us, event | category | flops | bytes accessed | tf_op | source)
XLA Modules:
  0.0 160.4 jit_solution(9395753211814944981)
XLA Ops:
  0.6 146.9 %shard_map.86 = (bf16[6,2,4,64,512]{4,3,2,1,0:T(8,128)(2,1)}, bf16[512,512]{1,0:T(8,128)(2,1)}) custom-call(s32[3]{0:T(128)} %roots_ref.1, bf16[512,1024]{1,0:T(8,128)(2,1)} %emb_ref.1, bf16[1024,3072]{1,0:T(8,128)(2,1)} %omega_ref.1, f32[1,3072]{1,0:T(1,128)} %bitcast.8, s32[1,3072]{1,0:T(1,128)} %bitcast.9, bf16[2,2,4,64,1024]{4,3,2,1,0:T(8,128)(2,1)} %bitcast.7, ...), custom_call_target="tpu_custom_call" | custom-call | flops 16106127360 | bytes 20971520 | tf_op jit(solution)/shard_map/pallas_call | solution.py:280
  147.5 7.3 %copy.9 = bf16[3,2,512,2,256]{4,3,2,1,0:T(2,128)(2,1)S(1)} copy(bf16[3,2,512,2,256]{2,4,1,3,0:T(8,128)(2,1)} %bitcast.6) | data formatting | bytes 6291456 | tf_op jit(solution)/shard_map/transpose | solution.py:321
  154.8 3.7 %reshape.11 = bf16[3,1024,512]{2,1,0:T(8,128)(2,1)} reshape(bf16[3,2,512,2,256]{4,3,2,1,0:T(2,128)(2,1)S(1)} %copy.9) | data formatting | bytes 6291456 | tf_op jit(solution)/shard_map/reshape | solution.py:322
  158.6 1.9 %copy.11 = bf16[512,512]{1,0:T(8,128)(2,1)} copy(bf16[512,512]{1,0:T(8,128)(2,1)} %get-tuple-element.9) | data formatting | bytes 1048576
